TPU v7x, 32 devices: a whole 2x2x4 slice. The times are simulated.
32 devices in a mesh: tm: 2 (over x), height: 4 (over y, core), mp: 4 (over z).
Axes of the slice: x: 2, y: 2, z: 4, core: 2. Of those that a mesh axis runs over, the one named last changes fastest.
Arguments:
- image_q: bfloat16 [2, 4, 384, 3072], P('tm', 'height', None, 'mp'), may hold values from -8 to 8
- image_kv: bfloat16 [2, 4, 2, 384, 3072], P('tm', 'height', None, None, 'mp'), may hold values from -8 to 8
- text_kv: bfloat16 [2, 256, 3072], P(None, 'tm', 'mp'), may hold values from -8 to 8
- residual: bfloat16 [2, 4, 384, 3072], P('tm', 'height', None, 'mp'), may hold values from -3 to 3
- out_weight: bfloat16 [3072, 3072], P('mp'), may hold values from -0.109375 to 0.109375
- out_gate: float32 [3072], P('mp'), may hold values from 0.5 to 2
- head_reach: int32 [24, 2], P('mp'), may hold values from 0 to 1, as said below
- tile_extent: int32 [2, 2, 4], replicated, may hold values from 1 to 8, as said below
Outputs:
- updated_tokens: bfloat16 [2, 4, 384, 3072], P('tm', 'height', None, 'mp')
Inputs may be any that keep to these rules, and one draw needn't show every extreme that they name: `head_reach`: in each column exactly 16 heads have reach 1, the others 0. `tile_extent`: valid frames are 6 except in the last tile row along time, where they are below 6; valid rows are 8 except in the last tile row along height, where they are below 8.
All inputs are finite; a program needn't handle non-finite values.
Results may differ from a plain program's by a relative error of at most 0.015.
Values may be sent and summed in bfloat16 or wider, within the bound.
A program may use at most 128 MiB of HBM per device.

v0:
```python
import math

import jax
import jax.numpy as jnp
from jax import lax
from jax.sharding import PartitionSpec as P

HD = 128
TXT = 256
TILE_F = 6
TILE_R = 8
TILE_C = 8


def with_halo(array, sides, width):
    for axis, dim in sides:
        devices, length = (lax.axis_size(axis), array.shape[dim])
        up = [(i, (i + 1) % devices) for i in range(devices - 1)]
        down = [(j, i) for i, j in up]
        last = lax.slice_in_dim(array, length - width, length, axis=dim)
        leading = lax.slice_in_dim(array, 0, width, axis=dim)
        before = lax.ppermute(last, axis, up)
        after = lax.ppermute(leading, axis, down)
        array = jnp.concatenate([before, array, after], axis=dim)
    return array


def token_masks(extent_pair):
    positions = jnp.arange(TILE_F * TILE_R * TILE_C, dtype=jnp.int32)
    frame_of = positions // (TILE_R * TILE_C)
    row_of = positions // TILE_C % TILE_R
    frame_ok = frame_of < extent_pair[0][..., None]
    row_ok = row_of < extent_pair[1][..., None]
    return jnp.logical_and(frame_ok, row_ok)


def extend_tiles(image_kv):
    return with_halo(image_kv, (("tm", 0), ("height", 1)), 1)


def per_device(image_q, image_kv, text_kv, residual, out_weight, out_gate, head_reach, tile_extent):
    tiles_local = image_q.shape[0]
    tile_len = image_q.shape[2]
    col_width = image_q.shape[3]
    heads_here = col_width // HD
    text_both = lax.all_gather(text_kv, "tm", axis=1, tiled=True)
    extended = extend_tiles(image_kv)
    time_start = lax.axis_index("tm") * tiles_local
    height_start = lax.axis_index("height")
    zero_index = jnp.int32(0)
    padded_ext = jnp.pad(tile_extent, ((0, 0), (1, 1), (1, 1)))
    local_ext = lax.dynamic_slice(
        padded_ext, (zero_index, time_start, height_start), (2, tiles_local + 2, 3)
    )
    key_valid = token_masks(local_ext)
    flat_valid = key_valid[1:-1, 1]
    flat_q = image_q.reshape(tiles_local, tile_len, col_width)
    offsets = jnp.abs(jnp.arange(3, dtype=jnp.int32) - 1)
    scale_factor = 1.0 / math.sqrt(HD)

    def one_tile(tile_index):
        key_rows = jnp.concatenate([extended[:, :, 0].reshape(-1, col_width), text_both[0]], axis=0)
        value_rows = jnp.concatenate(
            [extended[:, :, 1].reshape(-1, col_width), text_both[1]], axis=0
        )
        queries = lax.dynamic_index_in_dim(flat_q, tile_index, 0, keepdims=False)

        def one_head(packed):
            head_id, reaches = packed
            column_start = head_id * HD
            q_head = lax.dynamic_slice_in_dim(queries, column_start, HD, 1)
            k_head = lax.dynamic_slice_in_dim(key_rows, column_start, HD, 1)
            v_head = lax.dynamic_slice_in_dim(value_rows, column_start, HD, 1)
            image_ok = jnp.logical_and(key_valid, offsets[:, None, None] <= reaches[0])
            image_ok = jnp.logical_and(image_ok, offsets[None, :, None] <= reaches[1])
            allowed = jnp.concatenate([image_ok.reshape(-1), jnp.ones((TXT,), jnp.bool_)])
            scores = (
                lax.dot_general(
                    q_head, k_head, (((1,), (1,)), ((), ())), preferred_element_type=jnp.float32
                )
                * scale_factor
            )
            masked = jnp.where(allowed[None, :], scores, -1e30)
            top_score = jnp.max(masked, axis=1, keepdims=True)
            weights = jnp.where(allowed[None, :], jnp.exp(masked - top_score), 0.0)
            row_total = jnp.sum(weights, axis=1, keepdims=True)
            return (
                jnp.dot(weights.astype(jnp.bfloat16), v_head, preferred_element_type=jnp.float32)
                / row_total
            )

        per_head = lax.map(one_head, (jnp.arange(heads_here, dtype=jnp.int32), head_reach))
        joined = jnp.transpose(per_head, (1, 0, 2)).reshape(tile_len, col_width)
        valid_rows = lax.dynamic_index_in_dim(flat_valid, tile_index, 0, keepdims=False)
        return jnp.where(valid_rows[:, None], joined, 0.0).astype(jnp.bfloat16)

    attended = lax.map(one_tile, jnp.arange(tiles_local, dtype=jnp.int32))
    projected = jnp.dot(
        attended.reshape(-1, col_width), out_weight, preferred_element_type=jnp.float32
    )
    summed = lax.psum_scatter(
        projected.reshape(tiles_local, 1, tile_len, -1).astype(jnp.bfloat16),
        "mp",
        scatter_dimension=3,
        tiled=True,
    ).astype(jnp.float32)
    return (residual.astype(jnp.float32) + out_gate * summed).astype(jnp.bfloat16)


def solution(mesh):
    return jax.shard_map(
        per_device,
        mesh=mesh,
        in_specs=(
            P("tm", "height", None, "mp"),
            P("tm", "height", None, None, "mp"),
            P(None, "tm", "mp"),
            P("tm", "height", None, "mp"),
            P("mp", None),
            P("mp"),
            P("mp", None),
            P(),
        ),
        out_specs=P("tm", "height", None, "mp"),
        check_vma=False,
    )
```

profile of v0, /device:TPU:20, one launch (start us, length us, event | category | flops | bytes accessed | tf_op | source)
XLA Modules:
  0.0 228.7 jit_solution(3325906950139453624)
XLA Ops:
  6.5 3.6 %collective-permute-start = (bf16[1,1,2,384,768]{4,3,2,1,0:T(8,128)(2,1)}, bf16[1,1,2,384,768]{4,3,2,1,0:T(8,128)(2,1)S(1)}, u32[]{:S(2)}, u32[]{:S(2)}) collective-permute-start(bf16[1,1,2,384,768]{4,3,2,1,0:T(8,128)(2,1)} %param.11), channel_id=1, source_target_pairs={{0,16},{1,17},{2,18},{3,19},{4,20},{5,21},{6,22},{7,23},{8,24},{9,... | collective-permute-start | bytes 3538952 | tf_op jit(solution)/shard_map/ppermute | solution.py:22
  10.1 1.3 collective-permute-start.1
  11.4 24.1 %collective-permute-done = bf16[1,1,2,384,768]{4,3,2,1,0:T(8,128)(2,1)S(1)} collective-permute-done((bf16[1,1,2,384,768]{4,3,2,1,0:T(8,128)(2,1)}, bf16[1,1,2,384,768]{4,3,2,1,0:T(8,128)(2,1)S(1)}, u32[]{:S(2)}, u32[]{:S(2)}) %collective-permute-start) | collective-permute-done | bytes 1179680 | tf_op jit(solution)/shard_map/ppermute | solution.py:22
  35.7 1.4 constant_dynamic-update-slice_fusion.2
  37.0 2.7 %collective-permute-done.1 = bf16[1,1,2,384,768]{4,3,2,1,0:T(8,128)(2,1)S(1)} collective-permute-done((bf16[1,1,2,384,768]{4,3,2,1,0:T(8,128)(2,1)}, bf16[1,1,2,384,768]{4,3,2,1,0:T(8,128)(2,1)S(1)}, u32[]{:S(2)}, u32[]{:S(2)}) %collective-permute-start.1) | collective-permute-done | bytes 1179680 | tf_op jit(solution)/shard_map/ppermute | solution.py:23
  39.8 1.9 collective-permute-start.2
  41.7 3.6 %collective-permute-start.3 = (bf16[3,1,2,384,768]{4,3,2,1,0:T(8,128)(2,1)S(1)}, bf16[3,1,2,384,768]{4,3,2,1,0:T(8,128)(2,1)}, u32[]{:S(2)}, u32[]{:S(2)}) collective-permute-start(bf16[3,1,2,384,768]{4,3,2,1,0:T(8,128)(2,1)S(1)} %constant_dynamic-update-slice_fusion.1), channel_id=1, source_target_pairs={{4,0},{8,4},{12,8},{5,1},{9,5},{13,9},{6,2},{10,6},{14,10},{7,3},{... | collective-permute-start | bytes 10616840 | tf_op jit(solution)/shard_map/ppermute | solution.py:23
  45.5 0.6 slice.44
  46.6 1.7 and_reduce_fusion
  48.4 12.5 %all_gather.3 = bf16[2,256,768]{2,1,0:T(8,128)(2,1)S(1)} all-gather(bf16[2,128,768]{2,1,0:T(8,128)(2,1)} %param.12), channel_id=1, replica_groups=mesh['tm'=2,'height'=4,'mp'=4] {'tm'}, dimensions={1}, use_global_device_ids=true | all-gather | bytes 1179648 | tf_op jit(solution)/shard_map/all_gather | solution.py:46
  60.9 1.0 slice_bitcast_fusion
  61.9 20.8 %collective-permute-done.2 = bf16[3,1,2,384,768]{4,3,2,1,0:T(8,128)(2,1)} collective-permute-done((bf16[3,1,2,384,768]{4,3,2,1,0:T(8,128)(2,1)S(1)}, bf16[3,1,2,384,768]{4,3,2,1,0:T(8,128)(2,1)}, u32[]{:S(2)}, u32[]{:S(2)}) %collective-permute-start.2) | collective-permute-done | bytes 3538976 | tf_op jit(solution)/shard_map/ppermute | solution.py:22
  82.7 1.7 collective-permute-done.3
  84.3 8.2 %pad_maximum_fusion = bf16[3,3,2,384,768]{4,3,2,1,0:T(8,128)(2,1)} fusion(bf16[3,1,2,384,768]{4,3,2,1,0:T(8,128)(2,1)} %collective-permute-done.3, bf16[3,1,2,384,768]{4,3,2,1,0:T(8,128)(2,1)S(1)} %constant_dynamic-update-slice_fusion.1, bf16[3,1,2,384,768]{4,3,2,1,0:T(8,128)(2,1)} %collective-permute-done.2), kind=kLoop, calls=%fused_computation.26 | loop fusion | flops 10616832 | bytes 21233664 | tf_op jit(solution)/shard_map/concatenate | solution.py:24
  92.5 9.0 %fusion.39 = (bf16[3,3,1,384,768]{4,3,2,1,0:T(8,128)(2,1)}, bf16[3,3,1,384,768]{4,3,2,1,0:T(8,128)(2,1)}) fusion(bf16[3,3,2,384,768]{4,3,2,1,0:T(8,128)(2,1)} %pad_maximum_fusion), kind=kLoop, calls=%fused_computation.62 | loop fusion | bytes 21233664 | tf_op jit(solution)/shard_map/while/body/eval_jaxpr/slice | solution.py:64
  101.5 9.5 %pad_maximum_fusion.1 = (bf16[3712,768]{1,0:T(8,128)(2,1)}, bf16[3712,768]{1,0:T(8,128)(2,1)}) fusion(bf16[256,768]{1,0:T(8,128)(2,1)S(1)} %copy-done.1, bf16[3456,768]{1,0:T(8,128)(2,1)} %bitcast.35, bf16[256,768]{1,0:T(8,128)(2,1)S(1)} %copy-done, bf16[3456,768]{1,0:T(8,128)(2,1)} %bitcast.34), kind=kLoop, calls=%fused_computation.27 | loop fusion | flops 22806528 | bytes 22806528 | tf_op jit(solution)/shard_map/while/body/eval_jaxpr/concatenate | solution.py:62
  111.0 54.3 %while.19 = (s32[]{:T(128)}, bf16[6,384,128]{1,2,0:T(8,128)(2,1)S(1)}, s32[6,2]{0,1:T(2,128)S(1)}, s32[6]{0:T(128)S(1)}, bf16[384,768]{1,0:T(8,128)(2,1)}, /*ind...) while((s32[]{:T(128)}, ...), condition=%wide.region_3.4_spmd.clone.clone, body=%wide.region_0.3_spmd.clone.clone.sunk | while | flops 742752384 | bytes 19636056 | solution.py:92
  111.6 1.2 fusion.53
  112.9 0.6 dynamic_slice.60
  114.2 2.4 %fusion.55 = (f32[384]{0:T(512)S(1)}, f32[384,3712]{1,0:T(8,128)S(1)}) fusion(bf16[3712,768]{1,0:T(8,128)(2,1)} %get-tuple-element.288, s32[]{:T(128)S(6)} %select_n.100, bf16[384,768]{1,0:T(8,128)(2,1)} %get-tuple-element.287, pred[3712]{0:T(1024)(128)(4,1)S(1)} %concatenate.24), kind=kOutput, calls=%fused_computation.61.clone.1 | convolution fusion | flops 369180288 | bytes 6756480 | tf_op jit(solution)/shard_map/while/body/eval_jaxpr/while/body/eval_jaxpr/dot_general | solution.py:78
  116.6 1.2 fusion.56
  117.7 2.2 fusion.57
  120.7 1.2 fusion.53
  122.0 0.6 dynamic_slice.60
  123.2 2.4 %fusion.55 = (f32[384]{0:T(512)S(1)}, f32[384,3712]{1,0:T(8,128)S(1)}) fusion(bf16[3712,768]{1,0:T(8,128)(2,1)} %get-tuple-element.288, s32[]{:T(128)S(6)} %select_n.100, bf16[384,768]{1,0:T(8,128)(2,1)} %get-tuple-element.287, pred[3712]{0:T(1024)(128)(4,1)S(1)} %concatenate.24), kind=kOutput, calls=%fused_computation.61.clone.1 | convolution fusion | flops 369180288 | bytes 6756480 | tf_op jit(solution)/shard_map/while/body/eval_jaxpr/while/body/eval_jaxpr/dot_general | solution.py:78
  125.6 1.2 fusion.56
  126.8 2.2 fusion.57
  129.7 1.2 fusion.53
  131.1 0.6 dynamic_slice.60
  132.3 2.4 %fusion.55 = (f32[384]{0:T(512)S(1)}, f32[384,3712]{1,0:T(8,128)S(1)}) fusion(bf16[3712,768]{1,0:T(8,128)(2,1)} %get-tuple-element.288, s32[]{:T(128)S(6)} %select_n.100, bf16[384,768]{1,0:T(8,128)(2,1)} %get-tuple-element.287, pred[3712]{0:T(1024)(128)(4,1)S(1)} %concatenate.24), kind=kOutput, calls=%fused_computation.61.clone.1 | convolution fusion | flops 369180288 | bytes 6756480 | tf_op jit(solution)/shard_map/while/body/eval_jaxpr/while/body/eval_jaxpr/dot_general | solution.py:78
  134.7 1.2 fusion.56
  135.8 2.2 fusion.57
  138.8 1.2 fusion.53
  141.3 2.4 %fusion.55 = (f32[384]{0:T(512)S(1)}, f32[384,3712]{1,0:T(8,128)S(1)}) fusion(bf16[3712,768]{1,0:T(8,128)(2,1)} %get-tuple-element.288, s32[]{:T(128)S(6)} %select_n.100, bf16[384,768]{1,0:T(8,128)(2,1)} %get-tuple-element.287, pred[3712]{0:T(1024)(128)(4,1)S(1)} %concatenate.24), kind=kOutput, calls=%fused_computation.61.clone.1 | convolution fusion | flops 369180288 | bytes 6756480 | tf_op jit(solution)/shard_map/while/body/eval_jaxpr/while/body/eval_jaxpr/dot_general | solution.py:78
  143.7 1.2 fusion.56
  144.9 2.2 fusion.57
  147.8 1.2 fusion.53
  149.2 0.6 dynamic_slice.60
  150.4 2.4 %fusion.55 = (f32[384]{0:T(512)S(1)}, f32[384,3712]{1,0:T(8,128)S(1)}) fusion(bf16[3712,768]{1,0:T(8,128)(2,1)} %get-tuple-element.288, s32[]{:T(128)S(6)} %select_n.100, bf16[384,768]{1,0:T(8,128)(2,1)} %get-tuple-element.287, pred[3712]{0:T(1024)(128)(4,1)S(1)} %concatenate.24), kind=kOutput, calls=%fused_computation.61.clone.1 | convolution fusion | flops 369180288 | bytes 6756480 | tf_op jit(solution)/shard_map/while/body/eval_jaxpr/while/body/eval_jaxpr/dot_general | solution.py:78
  152.8 1.2 fusion.56
  154.0 2.2 fusion.57
  156.9 1.2 fusion.53
  159.5 2.4 %fusion.55 = (f32[384]{0:T(512)S(1)}, f32[384,3712]{1,0:T(8,128)S(1)}) fusion(bf16[3712,768]{1,0:T(8,128)(2,1)} %get-tuple-element.288, s32[]{:T(128)S(6)} %select_n.100, bf16[384,768]{1,0:T(8,128)(2,1)} %get-tuple-element.287, pred[3712]{0:T(1024)(128)(4,1)S(1)} %concatenate.24), kind=kOutput, calls=%fused_computation.61.clone.1 | convolution fusion | flops 369180288 | bytes 6756480 | tf_op jit(solution)/shard_map/while/body/eval_jaxpr/while/body/eval_jaxpr/dot_general | solution.py:78
  161.8 1.2 fusion.56
  163.0 2.2 fusion.57
  165.5 5.9 %fusion.27 = bf16[1,1,384,3072]{3,2,1,0:T(8,128)(2,1)} fusion(bf16[384,768]{0,1:T(8,128)(2,1)S(1)} %fusion.28, bf16[768,3072]{1,0:T(8,128)(2,1)} %param.14), kind=kOutput, calls=%fused_computation.30 | convolution fusion | flops 1813118976 | bytes 7667712 | tf_op jit(solution)/shard_map/dot_general | solution.py:98
  171.4 48.4 %reduce-scatter.2.cloned.1.call-done = bf16[1,1,384,768]{3,2,1,0:T(8,128)(2,1)} async-done(((bf16[1,1,384,3072]{3,2,1,0:T(8,128)(2,1)}), bf16[1,1,384,768]{3,2,1,0:T(8,128)(2,1)}) %reduce-scatter.2.cloned.1.call-update) | async-done | bytes 589840 | tf_op jit(solution)/shard_map/reduce_scatter | solution.py:101
  219.8 2.1 add_convert_fusion
  (70 shorter events, 7.3 us)
Async XLA Ops:
  6.5 38.8 %copy-start.7 = (s32[2,2,4]{2,1,0:T(2,128)S(1)}, s32[2,2,4]{2,1,0:T(2,128)}, u32[]{:S(2)}) copy-start(s32[2,2,4]{2,1,0:T(2,128)} %param.17) | copy-start | bytes 196
  6.5 213.3 %reduce-scatter.2.cloned.1.call-start = ((), (), s32[]{:S(2)}) async-start(), calls=%async_computation.1 | async-start | bytes 2949120 | tf_op jit(solution)/shard_map/reduce_scatter | solution.py:101
  6.5 29.0 %collective-permute-start = (bf16[1,1,2,384,768]{4,3,2,1,0:T(8,128)(2,1)}, bf16[1,1,2,384,768]{4,3,2,1,0:T(8,128)(2,1)S(1)}, u32[]{:S(2)}, u32[]{:S(2)}) collective-permute-start(bf16[1,1,2,384,768]{4,3,2,1,0:T(8,128)(2,1)} %param.11), channel_id=1, source_target_pairs={{0,16},{1,17},{2,18},{3,19},{4,20},{5,21},{6,22},{7,23},{8,24},{9,... | collective-permute-start | bytes 3538952 | tf_op jit(solution)/shard_map/ppermute | solution.py:22
  10.1 29.5 %collective-permute-start.1 = (bf16[1,1,2,384,768]{4,3,2,1,0:T(8,128)(2,1)}, bf16[1,1,2,384,768]{4,3,2,1,0:T(8,128)(2,1)S(1)}, u32[]{:S(2)}, u32[]{:S(2)}) collective-permute-start(bf16[1,1,2,384,768]{4,3,2,1,0:T(8,128)(2,1)} %param.11), channel_id=1, source_target_pairs={{16,0},{17,1},{18,2},{19,3},{20,4},{21,5},{22,6},{23,7},{24,8},{25... | collective-permute-start | bytes 3538952 | tf_op jit(solution)/shard_map/ppermute | solution.py:23
  39.8 42.9 %collective-permute-start.2 = (bf16[3,1,2,384,768]{4,3,2,1,0:T(8,128)(2,1)S(1)}, bf16[3,1,2,384,768]{4,3,2,1,0:T(8,128)(2,1)}, u32[]{:S(2)}, u32[]{:S(2)}) collective-permute-start(bf16[3,1,2,384,768]{4,3,2,1,0:T(8,128)(2,1)S(1)} %constant_dynamic-update-slice_fusion.1), channel_id=1, source_target_pairs={{0,4},{4,8},{8,12},{1,5},{5,9},{9,13},{2,6},{6,10},{10,14},{3,7},{... | collective-permute-start | bytes 10616840 | tf_op jit(solution)/shard_map/ppermute | solution.py:22
  41.7 42.6 %collective-permute-start.3 = (bf16[3,1,2,384,768]{4,3,2,1,0:T(8,128)(2,1)S(1)}, bf16[3,1,2,384,768]{4,3,2,1,0:T(8,128)(2,1)}, u32[]{:S(2)}, u32[]{:S(2)}) collective-permute-start(bf16[3,1,2,384,768]{4,3,2,1,0:T(8,128)(2,1)S(1)} %constant_dynamic-update-slice_fusion.1), channel_id=1, source_target_pairs={{4,0},{8,4},{12,8},{5,1},{9,5},{13,9},{6,2},{10,6},{14,10},{7,3},{... | collective-permute-start | bytes 10616840 | tf_op jit(solution)/shard_map/ppermute | solution.py:23
  92.5 9.0 %copy-start = (bf16[256,768]{1,0:T(8,128)(2,1)S(1)}, bf16[256,768]{1,0:T(8,128)(2,1)}, u32[]{:S(2)}) copy-start(bf16[256,768]{1,0:T(8,128)(2,1)} %get-tuple-element.164) | copy-start | bytes 1179652
  92.5 9.0 %copy-start.1 = (bf16[256,768]{1,0:T(8,128)(2,1)S(1)}, bf16[256,768]{1,0:T(8,128)(2,1)}, u32[]{:S(2)}) copy-start(bf16[256,768]{1,0:T(8,128)(2,1)} %get-tuple-element.165) | copy-start | bytes 1179652
  101.5 9.5 %copy-start.3 = (bf16[6,384,128]{1,2,0:T(8,128)(2,1)S(1)}, bf16[6,384,128]{1,2,0:T(8,128)(2,1)}, u32[]{:S(2)}) copy-start(bf16[6,384,128]{1,2,0:T(8,128)(2,1)} %custom-call.1) | copy-start | bytes 1769476
  101.5 9.5 %copy-start.4 = (s32[6,2]{0,1:T(2,128)S(1)}, s32[6,2]{0,1:T(2,128)}, u32[]{:S(2)}) copy-start(s32[6,2]{0,1:T(2,128)} %param.16) | copy-start | bytes 148
  111.0 54.3 %copy-start.6 = (pred[384]{0:T(512)(128)(4,1)S(1)}, pred[384]{0:T(512)(128)(4,1)}, u32[]{:S(2)}) copy-start(pred[384]{0:T(512)(128)(4,1)} %and_reduce_fusion) | copy-start | bytes 1156
  165.5 54.3 %copy-start.2 = (bf16[1,1,384,768]{3,2,1,0:T(8,128)(2,1)S(1)}, bf16[1,1,384,768]{3,2,1,0:T(8,128)(2,1)}, u32[]{:S(2)}) copy-start(bf16[1,1,384,768]{3,2,1,0:T(8,128)(2,1)} %param.13) | copy-start | bytes 1769476
  165.5 54.3 %copy-start.5 = (f32[768]{0:T(1024)S(1)}, f32[768]{0:T(1024)}, u32[]{:S(2)}) copy-start(f32[768]{0:T(1024)} %param.15) | copy-start | bytes 9220
Sparse Core Ops, SparseCore 0:
  171.6 48.2 reduce-scatter.1
where the time goes:
time: 232 us; the launch traced here: 229 us
  waiting for transfers between devices  97.7 us (42%)
  other arithmetic  36.3 us (16%)
  matrix products  33.1 us (14%)
  local copies, waits for them, and re-layouts  20.9 us (9%)
  between operations  13.5 us (6%)
  blocking collectives  12.5 us (5%)
  starting transfers between devices  10.5 us (5%)
  loops' own time  4.28 us (2%)
    reduce_scatter x1, waiting for transfers between devices, per_device(): lax.psum_scatter(projected.reshape(tiles_local, 1, tile_len, -1).astype(j...  48.4 us
    ppermute x2, waiting for transfers between devices, with_halo(): before = lax.ppermute(last, axis, up)  45 us
    dot_general x6, matrix products, one_head(): lax.dot_general(q_head, k_head, (((1,), (1,)), ((), ())), preferred_eleme...  14.3 us
    dot_general x6, matrix products, one_head(): jnp.dot(weights.astype(jnp.bfloat16), v_head, preferred_element_type=jnp....  12.9 us
    all_gather x1, blocking collectives, per_device(): text_both = lax.all_gather(text_kv, 'tm', axis=1, tiled=True)  12.5 us
    concatenate x1, other arithmetic, one_tile(): jnp.concatenate([extended[:, :, 0].reshape(-1, col_width), text_both[0]],...  9.48 us
    slice x1, local copies, waits for them, and re-layouts, one_tile(): extended[:, :, 1].reshape(-1, col_width)  8.97 us
    concatenate x1, other arithmetic, with_halo(): array = jnp.concatenate([before, array, after], axis=dim)  8.19 us
  transfers between devices with their start and end apart: 5, of which 5 were waited for; matrix products, arithmetic and copies ran while one was open for 2% of the time, Pallas kernels for 0%

commit v1 on v0

v1 whole, which is shorter than its diff:
```python
import functools
import math

import jax
import jax.numpy as jnp
from jax import lax
from jax.experimental import pallas as pl
from jax.experimental.pallas import tpu as pltpu
from jax.sharding import PartitionSpec as P

HD = 128
TILE_F = 6
TILE_R = 8
TILE_C = 8
HEADS_PER_CHUNK = 2
ROW_CHUNKS = 3
NEG = -1e30
MESH = pl.DeviceIdType.MESH


def kernel(
    sizes,
    q_ref, kv_hbm, text_hbm, res_hbm, w_hbm, gate_ref, reach_ref, extent_ref,
    out_ref,
    buf, txt, w_ref, res_ref, att, acc, top, total, final,
    right_out, right_in, left_out, left_in,
    local_sem, text_send, text_recv, text_fsend, text_frecv,
    time_send, high_send, kv_recv,
    right_send, right_recv, left_send, left_recv,
):
    tm, height, mp, slots = sizes
    tile, width = q_ref.shape
    heads = width // HD
    chunks = heads // HEADS_PER_CHUNK
    chunk_width = HEADS_PER_CHUNK * HD
    text_rows = text_hbm.shape[1]
    t, h, m = lax.axis_index("tm"), lax.axis_index("height"), lax.axis_index("mp")
    scale = math.log2(math.e) / math.sqrt(HD)

    if tm == 1:
        times = []
    elif tm == 2:
        times = [(1, 1 - t, t >= 0, 1)]
    else:
        times = [(1, t - 1, t > 0, 2), (2, t + 1, t < tm - 1, 1)]
    highs = [(0, h - 1, h > 0, 2), (2, h + 1, h < height - 1, 0)]
    pair = h + 1 - 2 * (h % 2)
    parity = h % 2

    own_kv = pltpu.make_async_copy(kv_hbm, buf.at[0, 1], local_sem.at[0])
    own_rows = pl.ds(pl.multiple_of(t * text_rows, text_rows), text_rows)
    own_text = pltpu.make_async_copy(text_hbm, txt.at[:, own_rows], local_sem.at[1])
    w_copy = pltpu.make_async_copy(w_hbm, w_ref, local_sem.at[2])
    res_copy = pltpu.make_async_copy(res_hbm, res_ref, local_sem.at[3])
    own_kv.start()
    own_text.start()

    barrier = pltpu.get_barrier_semaphore()
    for step in range(1, tm):
        pl.semaphore_signal(
            barrier, inc=1, device_id={"tm": (t + step) % tm}, device_id_type=MESH
        )
    line = [("height", h - 1, h > 0), ("height", h + 1, h < height - 1),
            ("mp", m - 1, m > 0), ("mp", m + 1, m < mp - 1)]
    for axis, peer, there in line:
        @pl.when(there)
        def _(axis=axis, peer=peer):
            pl.semaphore_signal(
                barrier, inc=1, device_id={axis: peer}, device_id_type=MESH
            )
    count = tm - 1
    for _, _, there in line:
        count = count + there.astype(jnp.int32)
    pl.semaphore_wait(barrier, count)

    def cols_of(c):
        return pl.ds(c * chunk_width, chunk_width)

    def text_copy(step):
        peer = (t + step) % tm
        return pltpu.make_async_remote_copy(
            src_ref=text_hbm.at[parity],
            dst_ref=txt.at[parity, own_rows],
            send_sem=text_send.at[step], recv_sem=text_recv.at[step],
            device_id={"tm": peer}, device_id_type=MESH,
        )

    def text_arrived(step, kind):
        rows = pl.ds(pl.multiple_of(((t + tm - step) % tm) * text_rows, text_rows), text_rows)
        return txt.at[kind, rows]

    def text_landed(step):
        ref = text_arrived(step, parity)
        return pltpu.make_async_remote_copy(
            src_ref=ref, dst_ref=ref,
            send_sem=text_send.at[step], recv_sem=text_recv.at[step],
            device_id={"tm": (t + step) % tm}, device_id_type=MESH,
        )

    def text_forward(step, kind):
        ref = text_arrived(step, kind)
        return pltpu.make_async_remote_copy(
            src_ref=ref, dst_ref=ref,
            send_sem=text_fsend.at[step], recv_sem=text_frecv.at[step],
            device_id={"height": pair}, device_id_type=MESH,
        )

    def time_copy(c, slot, peer, there_slot):
        return pltpu.make_async_remote_copy(
            src_ref=kv_hbm.at[:, :, cols_of(c)],
            dst_ref=buf.at[there_slot, 1, :, :, cols_of(c)],
            send_sem=time_send.at[slot, c], recv_sem=kv_recv.at[there_slot, 1, c],
            device_id={"tm": peer}, device_id_type=MESH,
        )

    def high_copy(c, slot, side, peer, there_side):
        src = kv_hbm if slot == 0 else buf.at[slot, 1]
        return pltpu.make_async_remote_copy(
            src_ref=src.at[:, :, cols_of(c)],
            dst_ref=buf.at[slot, there_side, :, :, cols_of(c)],
            send_sem=high_send.at[slot, side, c],
            recv_sem=kv_recv.at[slot, there_side, c],
            device_id={"height": peer}, device_id_type=MESH,
        )

    def wait_landed(c, slot, side, axis, peer):
        ref = buf.at[slot, side, :, :, cols_of(c)]
        pltpu.make_async_remote_copy(
            src_ref=ref, dst_ref=ref,
            send_sem=high_send.at[slot, 0, c], recv_sem=kv_recv.at[slot, side, c],
            device_id={axis: peer}, device_id_type=MESH,
        ).wait_recv()

    for step in range(1, tm):
        text_copy(step).start()
    for c in range(chunks):
        for slot, peer, there, there_slot in times:
            @pl.when(there)
            def _(c=c, slot=slot, peer=peer, there_slot=there_slot):
                time_copy(c, slot, peer, there_slot).start()
        for side, peer, there, there_side in highs:
            @pl.when(there)
            def _(c=c, side=side, peer=peer, there_side=there_side):
                high_copy(c, 0, side, peer, there_side).start()
    w_copy.start()
    res_copy.start()

    position = lax.broadcasted_iota(jnp.int32, (1, tile), 1)
    frame_of = position // (TILE_R * TILE_C)
    row_of = position // TILE_C % TILE_R

    def bias_of(head, slot, side):
        dt = 0 if slot == 0 else 1
        dh = 0 if side == 1 else 1
        if slot == 0:
            t2 = t
        elif tm == 2:
            t2 = 1 - t
        else:
            t2 = t + (2 * slot - 3)
        h2 = h + side - 1
        frames = extent_ref[0, t2, h2]
        rows = extent_ref[1, t2, h2]
        near = jnp.logical_and(reach_ref[head, 0] >= dt, reach_ref[head, 1] >= dh)
        frames = jnp.where(near, frames, 0)
        ok = jnp.logical_and(frame_of < frames, row_of < rows)
        return jnp.where(ok, 0.0, NEG)

    def piece(head, k_of, v_of, bias, first=False):
        cols = pl.ds(pl.multiple_of(head * HD, HD), HD)
        s = lax.dot_general(
            q_ref[:, cols], k_of(cols), (((1,), (1,)), ((), ())),
            preferred_element_type=jnp.float32,
        ) * scale
        if bias is not None:
            s = s + bias
        peak = jnp.max(s, axis=1, keepdims=True)
        if not first:
            old = top[head]
            peak = jnp.maximum(peak, old)
        p = jnp.exp2(s - peak)
        row_sum = jnp.sum(p, axis=1, keepdims=True)
        pv = jnp.dot(p.astype(jnp.bfloat16), v_of(cols), preferred_element_type=jnp.float32)
        if not first:
            alpha = jnp.exp2(old - peak)
            row_sum = row_sum + alpha * total[head]
            pv = pv + alpha * acc[head]
        top[head] = peak
        total[head] = row_sum
        acc[head] = pv

    def image_piece(head, slot, side, first=False):
        piece(
            head,
            lambda cols: buf[slot, side, 0, :, cols],
            lambda cols: buf[slot, side, 1, :, cols],
            bias_of(head, slot, side), first,
        )

    own_kv.wait()

    @pl.loop(0, heads)
    def _(head):
        image_piece(head, 0, 1, True)

    for step in range(1, tm):
        text_landed(step).wait_recv()
        text_forward(step, parity).start()
    own_text.wait()
    for step in range(1, tm):
        text_forward(step, 1 - parity).wait_recv()

    @pl.loop(0, heads)
    def _(head):
        piece(head, lambda cols: txt[0, :, cols], lambda cols: txt[1, :, cols], None)

    def heads_of(c, slot, side):
        @pl.loop(c * HEADS_PER_CHUNK, (c + 1) * HEADS_PER_CHUNK)
        def _(head):
            image_piece(head, slot, side)

    query = lax.broadcasted_iota(jnp.int32, (tile, 1), 0)
    query_ok = jnp.logical_and(
        query // (TILE_R * TILE_C) < extent_ref[0, t, h],
        query // TILE_C % TILE_R < extent_ref[1, t, h],
    )

    def corners(c):
        for slot, _, there, _ in times:
            for side, peer, near, _ in highs:
                @pl.when(jnp.logical_and(there, near))
                def _(slot=slot, side=side, peer=peer):
                    wait_landed(c, slot, side, "height", peer)
                    heads_of(c, slot, side)

        @pl.loop(c * HEADS_PER_CHUNK, (c + 1) * HEADS_PER_CHUNK)
        def _(head):
            value = jnp.where(query_ok, acc[head] / total[head], 0.0)
            cols = pl.ds(pl.multiple_of(head * HD, HD), HD)
            att[:, cols] = value.astype(jnp.bfloat16)

    for c in range(chunks):
        for side, peer, there, _ in highs:
            @pl.when(there)
            def _(c=c, side=side, peer=peer):
                wait_landed(c, 0, side, "height", peer)
                heads_of(c, 0, side)
        for slot, peer, there, _ in times:
            @pl.when(there)
            def _(c=c, slot=slot, peer=peer):
                wait_landed(c, slot, 1, "tm", peer)
                for side, high_peer, near, there_side in highs:
                    @pl.when(near)
                    def _(side=side, high_peer=high_peer, there_side=there_side):
                        high_copy(c, slot, side, high_peer, there_side).start()
                heads_of(c, slot, 1)
        if c > 0:
            corners(c - 1)
    corners(chunks - 1)

    w_copy.wait()
    step_rows = tile // ROW_CHUNKS
    block = w_ref.shape[1] // mp

    def rows_of(r):
        return pl.ds(pl.multiple_of(r * step_rows, step_rows), step_rows)

    def part(d, r):
        if isinstance(d, int):
            columns = pl.ds(d * block, block)
        else:
            columns = pl.ds(pl.multiple_of(d * block, block), block)
        return jnp.dot(att[rows_of(r), :], w_ref[:, columns], preferred_element_type=jnp.float32)

    def right_copy(d, r):
        return pltpu.make_async_remote_copy(
            src_ref=right_out.at[d, rows_of(r)], dst_ref=right_in.at[d, rows_of(r)],
            send_sem=right_send.at[d, r], recv_sem=right_recv.at[d, r],
            device_id={"mp": m + 1}, device_id_type=MESH,
        )

    def left_copy(d, r):
        return pltpu.make_async_remote_copy(
            src_ref=left_out.at[d, rows_of(r)], dst_ref=left_in.at[d, rows_of(r)],
            send_sem=left_send.at[d, r], recv_sem=left_recv.at[d, r],
            device_id={"mp": m - 1}, device_id_type=MESH,
        )

    for k in range(mp - 1):
        @pl.loop(0, ROW_CHUNKS)
        def _(r, k=k):
            d = mp - 1 - k
            for dest, sends, inner, out, arrived, copy in (
                (d, m < d, m > 0, right_out, right_in, right_copy),
                (k, m > k, m < mp - 1, left_out, left_in, left_copy),
            ):
                @pl.when(jnp.logical_and(sends, jnp.logical_not(inner)))
                def _(dest=dest, out=out, copy=copy):
                    out[dest, rows_of(r), :] = part(dest, r).astype(jnp.bfloat16)
                    copy(dest, r).start()

                @pl.when(jnp.logical_and(sends, inner))
                def _(dest=dest, out=out, arrived=arrived, copy=copy):
                    value = part(dest, r)
                    copy(dest, r).wait_recv()
                    value = value + arrived[dest, rows_of(r), :].astype(jnp.float32)
                    out[dest, rows_of(r), :] = value.astype(jnp.bfloat16)
                    copy(dest, r).start()

    res_copy.wait()

    @pl.loop(0, ROW_CHUNKS)
    def _(r):
        final[...] = part(m, r)
        for arrived, sem, side, there in (
            (right_in, right_recv, -1, m > 0), (left_in, left_recv, 1, m < mp - 1)
        ):
            @pl.when(there)
            def _(arrived=arrived, sem=sem, side=side):
                ref = arrived.at[m, rows_of(r)]
                pltpu.make_async_remote_copy(
                    src_ref=ref, dst_ref=ref,
                    send_sem=local_sem.at[0], recv_sem=sem.at[m, r],
                    device_id={"mp": m + side}, device_id_type=MESH,
                ).wait_recv()
                final[...] += arrived[m, rows_of(r), :].astype(jnp.float32)
        value = res_ref[rows_of(r), :].astype(jnp.float32) + gate_ref[...] * final[...]
        out_ref[rows_of(r), :] = value.astype(jnp.bfloat16)

    for step in range(1, tm):
        text_copy(step).wait_send()
        text_forward(step, parity).wait_send()
    for c in range(chunks):
        for slot, peer, there, there_slot in times:
            @pl.when(there)
            def _(c=c, slot=slot, peer=peer, there_slot=there_slot):
                time_copy(c, slot, peer, there_slot).wait_send()
        for side, peer, near, there_side in highs:
            @pl.when(near)
            def _(c=c, side=side, peer=peer, there_side=there_side):
                high_copy(c, 0, side, peer, there_side).wait_send()
                for slot, _, there, _ in times:
                    @pl.when(there)
                    def _(slot=slot):
                        high_copy(c, slot, side, peer, there_side).wait_send()
    for k in range(mp - 1):
        @pl.loop(0, ROW_CHUNKS)
        def _(r, k=k):
            @pl.when(m < mp - 1 - k)
            def _():
                right_copy(mp - 1 - k, r).wait_send()

            @pl.when(m > k)
            def _():
                left_copy(k, r).wait_send()


def per_device(image_q, image_kv, text_kv, residual, out_weight, out_gate, head_reach, tile_extent):
    tm, height, mp = (lax.axis_size(axis) for axis in ("tm", "height", "mp"))
    tile, width = image_q.shape[2:]
    heads = width // HD
    chunks = heads // HEADS_PER_CHUNK
    slots = min(tm, 3)
    block = residual.shape[3]
    text = text_kv.shape[1] * tm
    half = jnp.bfloat16
    dma = pltpu.SemaphoreType.DMA
    vmem = pl.BlockSpec(memory_space=pltpu.VMEM)
    smem = pl.BlockSpec(memory_space=pltpu.SMEM)
    anywhere = pl.BlockSpec(memory_space=pl.ANY)
    result = pl.pallas_call(
        functools.partial(kernel, (tm, height, mp, slots)),
        out_shape=jax.ShapeDtypeStruct((tile, block), half),
        in_specs=[vmem, anywhere, anywhere, anywhere, anywhere, vmem, smem, smem],
        out_specs=vmem,
        scratch_shapes=[
            pltpu.VMEM((slots, 3, 2, tile, width), half),
            pltpu.VMEM((2, text, width), half),
            pltpu.VMEM(out_weight.shape, half),
            pltpu.VMEM((tile, block), half),
            pltpu.VMEM((tile, width), half),
            pltpu.VMEM((heads, tile, HD), jnp.float32),
            pltpu.VMEM((heads, tile, 1), jnp.float32),
            pltpu.VMEM((heads, tile, 1), jnp.float32),
            pltpu.VMEM((tile // ROW_CHUNKS, block), jnp.float32),
        ]
        + [pltpu.VMEM((mp, tile, block), half)] * 4
        + [
            dma((4,)), dma((tm,)), dma((tm,)), dma((tm,)), dma((tm,)),
            dma((slots, chunks)), dma((slots, 3, chunks)), dma((slots, 3, chunks)),
        ]
        + [dma((mp, ROW_CHUNKS))] * 4,
        compiler_params=pltpu.CompilerParams(
            collective_id=0, has_side_effects=True, vmem_limit_bytes=56 * 2**20
        ),
        cost_estimate=pl.CostEstimate(
            flops=6 * 10**9, bytes_accessed=8 * 10**6, transcendentals=6 * 10**6
        ),
    )(
        image_q.reshape(tile, width),
        image_kv.reshape(2, tile, width),
        text_kv,
        residual.reshape(tile, block),
        out_weight,
        out_gate.reshape(1, block),
        head_reach,
        tile_extent,
    )
    return result.reshape(residual.shape)


def solution(mesh):
    return jax.shard_map(
        per_device,
        mesh=mesh,
        in_specs=(
            P("tm", "height", None, "mp"),
            P("tm", "height", None, None, "mp"),
            P(None, "tm", "mp"),
            P("tm", "height", None, "mp"),
            P("mp", None),
            P("mp"),
            P("mp", None),
            P(),
        ),
        out_specs=P("tm", "height", None, "mp"),
        check_vma=False,
    )
```

time: 232 us -> 108 us (0.47); the launches traced: 229 us -> 108 us
  Pallas kernels: 0 us -> 103 us
  waiting for transfers between devices: 97.7 us -> 0 us
  other arithmetic: 36.3 us -> 0 us
  matrix products: 33.1 us -> 0 us
  local copies, waits for them, and re-layouts: 20.9 us -> 4.55 us
  between operations: 13.5 us -> 0.01 us
  blocking collectives: 12.5 us -> 0 us
  starting transfers between devices: 10.5 us -> 0 us
  loops' own time: 4.28 us -> 0 us
    pallas_call x0 -> x1, Pallas kernels: none -> 103 us  [per_device(): pl.pallas_call(functools.partial(kernel, (tm, height, mp, slots)), out_sh...]
    ppermute x4 -> x0, waiting for transfers between devices: 49.3 us -> none  [the longest x2 45 us: with_halo(): before = lax.ppermute(last, axis, up)]
    reduce_scatter x1 -> x0, waiting for transfers between devices: 48.4 us -> none  [per_device(): lax.psum_scatter(projected.reshape(tiles_local, 1, tile_len, -1).astype(j...]
    dot_general x13 -> x0, matrix products: 33.1 us -> none  [the longest x6 14.3 us: one_head(): lax.dot_general(q_head, k_head, (((1,), (1,)), ((), ())), preferred_eleme...]
    concatenate x2 -> x0, other arithmetic: 17.7 us -> none  [the longest x1 9.48 us: one_tile(): jnp.concatenate([extended[:, :, 0].reshape(-1, col_width), text_both[0]],...]
    slice x9 -> x0, local copies, waits for them, and re-layouts: 13.3 us -> none  [the longest x1 8.97 us: one_tile(): extended[:, :, 1].reshape(-1, col_width)]
    all_gather x1 -> x0, blocking collectives: 12.5 us -> none  [per_device(): text_both = lax.all_gather(text_kv, 'tm', axis=1, tiled=True)]
    ppermute x4 -> x0, starting transfers between devices: 10.4 us -> none  [the longest x2 5.51 us: with_halo(): before = lax.ppermute(last, axis, up)]
  transfers between devices with their start and end apart: 5 -> 0, of which waited for: 5 -> 0; matrix products, arithmetic and copies ran while one was open for 2% -> 0% of each run, Pallas kernels for 0% -> 0%
where the time goes in v1:
time: 108 us
  Pallas kernels  103 us (95%)
  local copies, waits for them, and re-layouts  4.55 us (4%)
    pallas_call x1, Pallas kernels, per_device(): pl.pallas_call(functools.partial(kernel, (tm, height, mp, slots)), out_sh...  103 us
    unnamed x2, local copies, waits for them, and re-layouts  3.27 us

profile of v1, /device:TPU:20, one launch (start us, length us, event | category | flops | bytes accessed | tf_op | source)
XLA Modules:
  0.0 108.0 jit_solution(3527981804608152084)
XLA Ops:
  0.0 1.3 %reshape.18.gate_ref = f32[1,768]{1,0:T(1,128)} reshape(f32[768]{0:T(1024)} %param.13) | data formatting | bytes 6144 | tf_op jit(solution)/shard_map/reshape | solution.py:405
  1.3 1.4 %copy.9.reach_ref = s32[6,2]{1,0:T(8,128)} copy(s32[6,2]{0,1:T(2,128)} %param.14) | data formatting | bytes 96 | tf_op args[6]
  2.6 103.5 %shard_map.82 = bf16[384,768]{1,0:T(8,128)(2,1)} custom-call(bf16[384,768]{1,0:T(8,128)(2,1)} %bitcast.6, bf16[2,384,768]{2,1,0:T(8,128)(2,1)} %bitcast.5, bf16[2,128,768]{2,1,0:T(8,128)(2,1)} %text_hbm.1, bf16[384,768]{1,0:T(8,128)(2,1)} %bitcast.7, bf16[768,3072]{1,0:T(8,128)(2,1)} %w_hbm.1, f32[1,768]{1,0:T(1,128)} %reshape.18.gate_ref, ...), custom_call_target="tpu_custom_call" | custom-call | flops 6000000000 | bytes 8000000 | tf_op jit(solution)/shard_map/pallas_call | solution.py:371
  106.1 1.9 %copy.11 = bf16[1,1,384,768]{3,2,1,0:T(8,128)(2,1)} copy(bf16[1,1,384,768]{3,2,1,0:T(8,128)(2,1)} %bitcast.4) | data formatting | bytes 1179648

commit v2 on v1

--- a/solution.py
+++ b/solution.py
@@ -12,8 +12,9 @@
 TILE_F = 6
 TILE_R = 8
 TILE_C = 8
-HEADS_PER_CHUNK = 2
+HEADS_PER_CHUNK = 1
 ROW_CHUNKS = 3
+LEAD = 2
 NEG = -1e30
 MESH = pl.DeviceIdType.MESH
 
@@ -161,7 +162,7 @@
         h2 = h + side - 1
         frames = extent_ref[0, t2, h2]
         rows = extent_ref[1, t2, h2]
-        near = jnp.logical_and(reach_ref[head, 0] >= dt, reach_ref[head, 1] >= dh)
+        near = jnp.logical_and(reach_ref[0, head] >= dt, reach_ref[1, head] >= dh)
         frames = jnp.where(near, frames, 0)
         ok = jnp.logical_and(frame_of < frames, row_of < rows)
         return jnp.where(ok, 0.0, NEG)
@@ -286,26 +287,40 @@
             device_id={"mp": m - 1}, device_id_type=MESH,
         )
 
-    for k in range(mp - 1):
-        @pl.loop(0, ROW_CHUNKS)
-        def _(r, k=k):
-            d = mp - 1 - k
-            for dest, sends, inner, out, arrived, copy in (
-                (d, m < d, m > 0, right_out, right_in, right_copy),
-                (k, m > k, m < mp - 1, left_out, left_in, left_copy),
-            ):
-                @pl.when(jnp.logical_and(sends, jnp.logical_not(inner)))
-                def _(dest=dest, out=out, copy=copy):
-                    out[dest, rows_of(r), :] = part(dest, r).astype(jnp.bfloat16)
-                    copy(dest, r).start()
-
-                @pl.when(jnp.logical_and(sends, inner))
-                def _(dest=dest, out=out, arrived=arrived, copy=copy):
-                    value = part(dest, r)
-                    copy(dest, r).wait_recv()
-                    value = value + arrived[dest, rows_of(r), :].astype(jnp.float32)
-                    out[dest, rows_of(r), :] = value.astype(jnp.bfloat16)
-                    copy(dest, r).start()
+    def stream_step(step, to_right):
+        k, r = step // ROW_CHUNKS, step % ROW_CHUNKS
+        if to_right:
+            d, out, arrived, copy = mp - 1 - k, right_out, right_in, right_copy
+            sends, inner = m < d, m > 0
+        else:
+            d, out, arrived, copy = k, left_out, left_in, left_copy
+            sends, inner = m > d, m < mp - 1
+
+        @pl.when(sends)
+        def _():
+            final[...] = part(d, r)
+
+            @pl.when(inner)
+            def _():
+                copy(d, r).wait_recv()
+                final[...] += arrived[d, rows_of(r), :].astype(jnp.float32)
+
+            out[d, rows_of(r), :] = final[...].astype(jnp.bfloat16)
+            copy(d, r).start()
+
+    steps = (mp - 1) * ROW_CHUNKS
+    for near, right_first in ((m < mp // 2, True), (m >= mp // 2, False)):
+        @pl.when(near)
+        def _(right_first=right_first):
+            @pl.loop(0, steps + LEAD)
+            def _(step):
+                @pl.when(step < steps)
+                def _():
+                    stream_step(step, right_first)
+
+                @pl.when(step >= LEAD)
+                def _():
+                    stream_step(step - LEAD, not right_first)
 
     res_copy.wait()
 
@@ -324,7 +339,7 @@
                     device_id={"mp": m + side}, device_id_type=MESH,
                 ).wait_recv()
                 final[...] += arrived[m, rows_of(r), :].astype(jnp.float32)
-        value = res_ref[rows_of(r), :].astype(jnp.float32) + gate_ref[...] * final[...]
+        value = res_ref[rows_of(r), :].astype(jnp.float32) + gate_ref[...][None, :] * final[...]
         out_ref[rows_of(r), :] = value.astype(jnp.bfloat16)
 
     for step in range(1, tm):
@@ -402,8 +417,8 @@
         text_kv,
         residual.reshape(tile, block),
         out_weight,
-        out_gate.reshape(1, block),
-        head_reach,
+        out_gate,
+        head_reach.T,
         tile_extent,
     )
     return result.reshape(residual.shape)

time: 108 us -> 84.1 us (0.78)
  Pallas kernels: 103 us -> 81.7 us
  local copies, waits for them, and re-layouts: 4.55 us -> 1.92 us
    pallas_call x1, Pallas kernels: 103 us -> 81.7 us  [per_device(): pl.pallas_call(functools.partial(kernel, (tm, height, mp, slots)), out_sh...]
    unnamed x2 -> x1, local copies, waits for them, and re-layouts: 3.27 us -> 1.92 us
    reshape x1 -> x0, local copies, waits for them, and re-layouts: 1.28 us -> none  [per_device(): out_gate.reshape(1, block)]
where the time goes in v2:
time: 84.1 us; the launch traced here: 83.6 us
  Pallas kernels  81.7 us (97%)
  local copies, waits for them, and re-layouts  1.92 us (2%)
    pallas_call x1, Pallas kernels, per_device(): pl.pallas_call(functools.partial(kernel, (tm, height, mp, slots)), out_sh...  81.7 us
    unnamed x1, local copies, waits for them, and re-layouts  1.92 us

profile of v2, /device:TPU:20, one launch (start us, length us, event | category | flops | bytes accessed | tf_op | source)
XLA Modules:
  0.0 83.6 jit_solution(7059724823572036293)
XLA Ops:
  0.0 81.7 %shard_map.82 = bf16[384,768]{1,0:T(8,128)(2,1)} custom-call(bf16[384,768]{1,0:T(8,128)(2,1)} %bitcast.7, bf16[2,384,768]{2,1,0:T(8,128)(2,1)} %bitcast.6, bf16[2,128,768]{2,1,0:T(8,128)(2,1)} %text_hbm.1, bf16[384,768]{1,0:T(8,128)(2,1)} %bitcast.8, bf16[768,3072]{1,0:T(8,128)(2,1)} %w_hbm.1, f32[768]{0:T(1024)} %gate_ref.1, s32[2,6]{1,0:T(2,128)} %bitcast.9, ...), custom_call_target="tpu_custom_call" | custom-call | flops 6000000000 | bytes 8000000 | tf_op jit(solution)/shard_map/pallas_call | solution.py:386
  81.7 1.9 %copy.10 = bf16[1,1,384,768]{3,2,1,0:T(8,128)(2,1)} copy(bf16[1,1,384,768]{3,2,1,0:T(8,128)(2,1)} %bitcast.5) | data formatting | bytes 1179648

commit v3 on v2

--- a/solution.py
+++ b/solution.py
@@ -13,8 +13,8 @@
 TILE_R = 8
 TILE_C = 8
 HEADS_PER_CHUNK = 1
-ROW_CHUNKS = 3
-LEAD = 2
+ROW_CHUNKS = 6
+LEAD = 4
 NEG = -1e30
 MESH = pl.DeviceIdType.MESH
 
@@ -48,6 +48,18 @@
     pair = h + 1 - 2 * (h % 2)
     parity = h % 2
 
+    short = tile - TILE_R * TILE_C
+    last_time = t == tm - 1
+
+    def by_rows(is_short, act):
+        @pl.when(is_short)
+        def _():
+            act(short)
+
+        @pl.when(jnp.logical_not(is_short))
+        def _():
+            act(tile)
+
     own_kv = pltpu.make_async_copy(kv_hbm, buf.at[0, 1], local_sem.at[0])
     own_rows = pl.ds(pl.multiple_of(t * text_rows, text_rows), text_rows)
     own_text = pltpu.make_async_copy(text_hbm, txt.at[:, own_rows], local_sem.at[1])
@@ -106,26 +118,26 @@
             device_id={"height": pair}, device_id_type=MESH,
         )
 
-    def time_copy(c, slot, peer, there_slot):
-        return pltpu.make_async_remote_copy(
-            src_ref=kv_hbm.at[:, :, cols_of(c)],
-            dst_ref=buf.at[there_slot, 1, :, :, cols_of(c)],
+    def time_copy(c, slot, peer, there_slot, rows):
+        return pltpu.make_async_remote_copy(
+            src_ref=kv_hbm.at[:, pl.ds(0, rows), cols_of(c)],
+            dst_ref=buf.at[there_slot, 1, :, pl.ds(0, rows), cols_of(c)],
             send_sem=time_send.at[slot, c], recv_sem=kv_recv.at[there_slot, 1, c],
             device_id={"tm": peer}, device_id_type=MESH,
         )
 
-    def high_copy(c, slot, side, peer, there_side):
+    def high_copy(c, slot, side, peer, there_side, rows):
         src = kv_hbm if slot == 0 else buf.at[slot, 1]
         return pltpu.make_async_remote_copy(
-            src_ref=src.at[:, :, cols_of(c)],
-            dst_ref=buf.at[slot, there_side, :, :, cols_of(c)],
+            src_ref=src.at[:, pl.ds(0, rows), cols_of(c)],
+            dst_ref=buf.at[slot, there_side, :, pl.ds(0, rows), cols_of(c)],
             send_sem=high_send.at[slot, side, c],
             recv_sem=kv_recv.at[slot, there_side, c],
             device_id={"height": peer}, device_id_type=MESH,
         )
 
-    def wait_landed(c, slot, side, axis, peer):
-        ref = buf.at[slot, side, :, :, cols_of(c)]
+    def wait_landed(c, slot, side, axis, peer, rows):
+        ref = buf.at[slot, side, :, pl.ds(0, rows), cols_of(c)]
         pltpu.make_async_remote_copy(
             src_ref=ref, dst_ref=ref,
             send_sem=high_send.at[slot, 0, c], recv_sem=kv_recv.at[slot, side, c],
@@ -138,13 +150,22 @@
         for slot, peer, there, there_slot in times:
             @pl.when(there)
             def _(c=c, slot=slot, peer=peer, there_slot=there_slot):
-                time_copy(c, slot, peer, there_slot).start()
+                by_rows(
+                    last_time, lambda n: time_copy(c, slot, peer, there_slot, n).start()
+                )
         for side, peer, there, there_side in highs:
             @pl.when(there)
             def _(c=c, side=side, peer=peer, there_side=there_side):
-                high_copy(c, 0, side, peer, there_side).start()
+                high_copy(c, 0, side, peer, there_side, tile).start()
     w_copy.start()
     res_copy.start()
+    for slot, peer, there, _ in times:
+        @pl.when(jnp.logical_and(there, peer == tm - 1))
+        def _(slot=slot):
+            for side in range(3):
+                buf[slot, side, :, short:, :] = jnp.zeros(
+                    (2, tile - short, width), jnp.bfloat16
+                )
 
     position = lax.broadcasted_iota(jnp.int32, (1, tile), 1)
     frame_of = position // (TILE_R * TILE_C)
@@ -227,11 +248,14 @@
     )
 
     def corners(c):
-        for slot, _, there, _ in times:
+        for slot, time_peer, there, _ in times:
             for side, peer, near, _ in highs:
                 @pl.when(jnp.logical_and(there, near))
-                def _(slot=slot, side=side, peer=peer):
-                    wait_landed(c, slot, side, "height", peer)
+                def _(slot=slot, side=side, peer=peer, time_peer=time_peer):
+                    by_rows(
+                        time_peer == tm - 1,
+                        lambda n: wait_landed(c, slot, side, "height", peer, n),
+                    )
                     heads_of(c, slot, side)
 
         @pl.loop(c * HEADS_PER_CHUNK, (c + 1) * HEADS_PER_CHUNK)
@@ -244,16 +268,23 @@
         for side, peer, there, _ in highs:
             @pl.when(there)
             def _(c=c, side=side, peer=peer):
-                wait_landed(c, 0, side, "height", peer)
+                wait_landed(c, 0, side, "height", peer, tile)
                 heads_of(c, 0, side)
         for slot, peer, there, _ in times:
             @pl.when(there)
             def _(c=c, slot=slot, peer=peer):
-                wait_landed(c, slot, 1, "tm", peer)
+                by_rows(
+                    peer == tm - 1, lambda n: wait_landed(c, slot, 1, "tm", peer, n)
+                )
                 for side, high_peer, near, there_side in highs:
                     @pl.when(near)
                     def _(side=side, high_peer=high_peer, there_side=there_side):
-                        high_copy(c, slot, side, high_peer, there_side).start()
+                        by_rows(
+                            peer == tm - 1,
+                            lambda n: high_copy(
+                                c, slot, side, high_peer, there_side, n
+                            ).start(),
+                        )
                 heads_of(c, slot, 1)
         if c > 0:
             corners(c - 1)
@@ -261,6 +292,7 @@
 
     w_copy.wait()
     step_rows = tile // ROW_CHUNKS
+    live = jnp.where(last_time, pl.cdiv(short, step_rows), ROW_CHUNKS)
     block = w_ref.shape[1] // mp
 
     def rows_of(r):
@@ -296,7 +328,7 @@
             d, out, arrived, copy = k, left_out, left_in, left_copy
             sends, inner = m > d, m < mp - 1
 
-        @pl.when(sends)
+        @pl.when(jnp.logical_and(sends, r < live))
         def _():
             final[...] = part(d, r)
 
@@ -330,7 +362,7 @@
         for arrived, sem, side, there in (
             (right_in, right_recv, -1, m > 0), (left_in, left_recv, 1, m < mp - 1)
         ):
-            @pl.when(there)
+            @pl.when(jnp.logical_and(there, r < live))
             def _(arrived=arrived, sem=sem, side=side):
                 ref = arrived.at[m, rows_of(r)]
                 pltpu.make_async_remote_copy(
@@ -349,23 +381,30 @@
         for slot, peer, there, there_slot in times:
             @pl.when(there)
             def _(c=c, slot=slot, peer=peer, there_slot=there_slot):
-                time_copy(c, slot, peer, there_slot).wait_send()
+                by_rows(
+                    last_time, lambda n: time_copy(c, slot, peer, there_slot, n).wait_send()
+                )
         for side, peer, near, there_side in highs:
             @pl.when(near)
             def _(c=c, side=side, peer=peer, there_side=there_side):
-                high_copy(c, 0, side, peer, there_side).wait_send()
-                for slot, _, there, _ in times:
+                high_copy(c, 0, side, peer, there_side, tile).wait_send()
+                for slot, time_peer, there, _ in times:
                     @pl.when(there)
-                    def _(slot=slot):
-                        high_copy(c, slot, side, peer, there_side).wait_send()
+                    def _(slot=slot, time_peer=time_peer):
+                        by_rows(
+                            time_peer == tm - 1,
+                            lambda n: high_copy(
+                                c, slot, side, peer, there_side, n
+                            ).wait_send(),
+                        )
     for k in range(mp - 1):
         @pl.loop(0, ROW_CHUNKS)
         def _(r, k=k):
-            @pl.when(m < mp - 1 - k)
+            @pl.when(jnp.logical_and(m < mp - 1 - k, r < live))
             def _():
                 right_copy(mp - 1 - k, r).wait_send()
 
-            @pl.when(m > k)
+            @pl.when(jnp.logical_and(m > k, r < live))
             def _():
                 left_copy(k, r).wait_send()
 

time: 84.1 us -> 84.6 us (level)
  no operation moved by 1% of the time
where the time goes in v3:
time: 84.6 us; the launch traced here: 83.8 us
  Pallas kernels  81.9 us (97%)
  local copies, waits for them, and re-layouts  1.92 us (2%)
    pallas_call x1, Pallas kernels, per_device(): pl.pallas_call(functools.partial(kernel, (tm, height, mp, slots)), out_sh...  81.9 us
    unnamed x1, local copies, waits for them, and re-layouts  1.92 us

profile of v3, /device:TPU:20, one launch (start us, length us, event | category | flops | bytes accessed | tf_op | source)
XLA Modules:
  0.0 83.8 jit_solution(16251811862807317846)
XLA Ops:
  0.0 81.9 %shard_map.82 = bf16[384,768]{1,0:T(8,128)(2,1)} custom-call(bf16[384,768]{1,0:T(8,128)(2,1)} %bitcast.7, bf16[2,384,768]{2,1,0:T(8,128)(2,1)} %bitcast.6, bf16[2,128,768]{2,1,0:T(8,128)(2,1)} %text_hbm.1, bf16[384,768]{1,0:T(8,128)(2,1)} %bitcast.8, bf16[768,3072]{1,0:T(8,128)(2,1)} %w_hbm.1, f32[768]{0:T(1024)} %gate_ref.1, s32[2,6]{1,0:T(2,128)} %bitcast.9, ...), custom_call_target="tpu_custom_call" | custom-call | flops 6000000000 | bytes 8000000 | tf_op jit(solution)/shard_map/pallas_call | solution.py:425
  81.9 1.9 %copy.10 = bf16[1,1,384,768]{3,2,1,0:T(8,128)(2,1)} copy(bf16[1,1,384,768]{3,2,1,0:T(8,128)(2,1)} %bitcast.5) | data formatting | bytes 1179648
